TPU v7x, 32 devices: a whole 2x2x4 slice. The times are simulated.
32 devices in a mesh: group: 2 (over y), row: 4 (over z), col: 2 (over x), tm: 2 (over core).
Axes of the slice: x: 2, y: 2, z: 4, core: 2. Of those that a mesh axis runs over, the one named last changes fastest.
Arguments:
- spectra: float32 [24, 32, 1024], P('tm', ('group', 'row', 'col')), parts along dimension 1, may hold values from -6 to 6
- station_block: int32 [32], P('group'), parts along dimension 0, may hold values from 0 to 15
- pair_mask: int32 [32, 16], P('group'), parts along dimension 0, may hold values 0 or 1
Outputs:
- linear_stack: float32 [32, 4, 2, 2, 1024], P(('group', 'row'), 'tm', 'col'), parts along dimension 0
- phase_stack: float32 [32, 4, 2, 2, 1024], P(('group', 'row'), 'tm', 'col'), parts along dimension 0
There are 2 independent parts, one for each index of `group`. A program takes and returns all parts, laid end to end along the dimension named above; each array names one. Nothing has to cross between parts.
All inputs are finite; a program needn't handle non-finite values.
Results may differ from a plain program's by a relative error of at most 0.0029.
Values sent between devices are 32-bit elements; how exact they have to be, the bound alone decides.
A program may use at most 64 MiB of HBM per device.

v0:
```python
import math

import jax
import jax.numpy as jnp
from jax import lax
from jax.sharding import PartitionSpec as P


def build_transform(bin_count):
    lag_count = 2 * bin_count
    phase_index = (
        jnp.arange(bin_count, dtype=jnp.int32)[:, None]
        * jnp.arange(lag_count, dtype=jnp.int32)[None, :]
        % lag_count
    )
    angles = phase_index.astype(jnp.float32) * (2.0 * math.pi / lag_count)
    cosine_values = jnp.cos(angles)
    sine_values = jnp.sin(angles)
    upper_half = jnp.concatenate([cosine_values, sine_values], 1)
    lower_half = jnp.concatenate([-sine_values, cosine_values], 1)
    return (
        jnp.concatenate([upper_half, lower_half], 0) * (1.0 / (3.0 * math.sqrt(bin_count)))
    ).astype(jnp.bfloat16)


def window_terms(left_side, right_side, transform):
    bin_count = left_side.shape[1] // 2
    left_real, left_imag = (left_side[:, :bin_count], left_side[:, bin_count:])
    right_real, right_imag = (right_side[:, :bin_count], right_side[:, bin_count:])
    real_cross = left_real[:, None, :] * right_real[None] + left_imag[:, None, :] * right_imag[None]
    imag_cross = left_imag[:, None, :] * right_real[None] - left_real[:, None, :] * right_imag[None]
    cross_spectra = jnp.concatenate([real_cross, imag_cross], -1).astype(jnp.bfloat16)
    cross_spectra = cross_spectra.reshape(left_side.shape[0] * right_side.shape[0], 2 * bin_count)
    analytic = jnp.dot(cross_spectra, transform, preferred_element_type=jnp.float32)
    lag_count = transform.shape[1] // 2
    real_part, imag_part = (analytic[:, :lag_count], analytic[:, lag_count:])
    magnitude = jnp.maximum(jnp.sqrt(real_part * real_part + imag_part * imag_part), 0.5)
    return (real_part, real_part / magnitude, imag_part / magnitude)


def stack_windows(left_side, right_side, transform):
    rows_first = left_side.shape[1]
    rows_second = right_side.shape[1]
    lag_count = transform.shape[1] // 2
    initial = (
        jnp.zeros((rows_first * rows_second, lag_count), jnp.float32),
        jnp.zeros((rows_first * rows_second, lag_count), jnp.float32),
        jnp.zeros((rows_first * rows_second, lag_count), jnp.float32),
    )

    def accumulate(totals, window):
        terms = window_terms(window[0], window[1], transform)
        return ((totals[0] + terms[0], totals[1] + terms[1], totals[2] + terms[2]), None)

    totals, ignored = lax.scan(accumulate, initial, (left_side, right_side))
    return tuple((part.reshape(rows_first, rows_second, lag_count) for part in totals))


def on_device(spectra, station_block, pair_mask):
    row_count = lax.axis_size("row")
    col_count = lax.axis_size("col")
    core_count = lax.axis_size("tm")
    owned = spectra.shape[1]
    transform = build_transform(spectra.shape[2] // 2)
    lag_count = transform.shape[1] // 2
    row_side = lax.all_gather(spectra, "col", axis=1, tiled=True)
    col_side = lax.all_gather(spectra, "row", axis=1, tiled=True)
    row_share = row_count // core_count
    core_index = lax.axis_index("tm")
    partial_value = stack_windows(row_side, col_side, transform)
    stack_sum, phase_real, phase_imag = (
        lax.psum_scatter(partial_value[0], "tm", scatter_dimension=1, tiled=True),
        lax.psum_scatter(partial_value[1], "tm", scatter_dimension=1, tiled=True),
        lax.psum_scatter(partial_value[2], "tm", scatter_dimension=1, tiled=True),
    )
    windows = spectra.shape[0] * core_count
    row_index = lax.axis_index("row")
    col_index = lax.axis_index("col")
    first_ids = lax.dynamic_slice_in_dim(
        station_block, row_index * col_count * owned, col_count * owned, 0
    )
    pieces = station_block.reshape(row_count, col_count, owned)
    pieces = lax.dynamic_slice_in_dim(pieces, core_index * row_share, row_share, 0)
    second_ids = lax.dynamic_slice_in_dim(pieces, col_index, 1, 1).reshape(-1)
    labels = jnp.arange(pair_mask.shape[0], dtype=jnp.int32)
    onehot_first = (first_ids[:, None] == labels[None, :]).astype(jnp.float32)
    onehot_second = (second_ids[:, None] == labels[None, :]).astype(jnp.float32)
    kept_pairs = jnp.dot(
        jnp.dot(onehot_first, pair_mask.astype(jnp.float32), preferred_element_type=jnp.float32),
        onehot_second.T,
        preferred_element_type=jnp.float32,
    )
    linear = kept_pairs[:, :, None] * stack_sum / windows
    weighted = linear * (phase_real * phase_real + phase_imag * phase_imag) / (windows * windows)
    out_shape = (col_count * owned, row_share, 1, owned, lag_count)
    return (linear.reshape(out_shape), weighted.reshape(out_shape))


def solution(mesh):
    in_specs = (P("tm", ("group", "row", "col"), None), P("group"), P("group", None))
    out_specs = (
        P(("group", "row"), "tm", "col", None, None),
        P(("group", "row"), "tm", "col", None, None),
    )
    return jax.shard_map(
        on_device, mesh=mesh, in_specs=in_specs, out_specs=out_specs, check_vma=False
    )
```

profile of v0, /device:TPU:1, one launch (start us, length us, event | category | flops | bytes accessed | tf_op | source)
XLA Modules:
  0.0 125.6 jit_solution(8625201763099643270)
XLA Ops:
  7.2 9.0 %fusion.17 = (f32[512,1024]{1,0:T(8,128)S(1)}, f32[512,1024]{1,0:T(8,128)}) fusion(), kind=kLoop, calls=%fused_computation.30 | loop fusion | flops 7340032 | bytes 4194304 | tf_op jit(solution)/shard_map/sin | solution.py:18
  16.2 8.6 %fusion.19 = f32[512,1024]{1,0:T(8,128)} fusion(), kind=kLoop, calls=%fused_computation.32 | loop fusion | flops 7864320 | bytes 2097152 | tf_op jit(solution)/shard_map/neg | solution.py:20
  24.8 15.3 %all_gather.7 = f32[12,8,1024]{2,0,1:T(8,128)S(1)} all-gather(f32[12,2,1024]{2,0,1:T(8,128)S(1)} %copy.5), channel_id=1, replica_groups=mesh['group'=2,'row'=4,'col'=2,'tm'=2] {'row'}, dimensions={1}, use_global_device_ids=true | all-gather | bytes 491520 | tf_op jit(solution)/shard_map/all_gather | solution.py:67
  40.1 4.5 %all_gather.6 = f32[12,4,1024]{2,0,1:T(8,128)S(1)} all-gather(f32[12,2,1024]{2,0,1:T(8,128)S(1)} %copy.5), channel_id=1, replica_groups=mesh['group'=2,'row'=4,'col'=2,'tm'=2] {'col'}, dimensions={1}, use_global_device_ids=true | all-gather | bytes 294912 | tf_op jit(solution)/shard_map/all_gather | solution.py:66
  44.6 7.6 %fusion.7 = bf16[1024,2048]{1,0:T(8,128)(2,1)} fusion(f32[512,1024]{1,0:T(8,128)} %get-tuple-element.106, f32[512,1024]{1,0:T(8,128)} %fusion.19, f32[512,1024]{1,0:T(8,128)S(1)} %get-tuple-element.105), kind=kLoop, calls=%fused_computation.18 | loop fusion | flops 10485760 | bytes 10485760 | tf_op jit(solution)/shard_map/convert_element_type | solution.py:23
  52.2 39.8 %while.15 = (s32[]{:T(128)}, f32[32,1024]{1,0:T(8,128)S(1)}, f32[32,1024]{1,0:T(8,128)S(1)}, f32[32,1024]{1,0:T(8,128)S(1)}, f32[12,4,1024]{2,0,1:T(8,128)S(1)},...) while((s32[]{:T(128)}, f32[32,1024]{1,0:T(8,128)S(1)}, ...), condition=%wide.region_1.2_spmd.clone, body=%wide.region_0.1_spmd.clone.sunk | while | flops 134873088 | bytes 5980271 | solution.py:55
  52.4 3.0 %fusion.44 = f32[32,2048]{1,0:T(8,128)S(1)} fusion(bf16[1024,2048]{1,0:T(8,128)(2,1)} %get-tuple-element.192, bf16[32,512]{1,0:T(8,128)(2,1)S(1)} %get-tuple-element.163, bf16[32,512]{1,0:T(8,128)(2,1)S(1)} %get-tuple-element.164), kind=kOutput, calls=%fused_computation.4.clone.1 | convolution fusion | flops 134348800 | bytes 4521984 | tf_op jit(solution)/shard_map/while/body/eval_jaxpr/dot_general | solution.py:34
  55.4 0.1 select_add_fusion.4
  55.7 3.0 %fusion.44 = f32[32,2048]{1,0:T(8,128)S(1)} fusion(bf16[1024,2048]{1,0:T(8,128)(2,1)} %get-tuple-element.192, bf16[32,512]{1,0:T(8,128)(2,1)S(1)} %get-tuple-element.163, bf16[32,512]{1,0:T(8,128)(2,1)S(1)} %get-tuple-element.164), kind=kOutput, calls=%fused_computation.4.clone.1 | convolution fusion | flops 134348800 | bytes 4521984 | tf_op jit(solution)/shard_map/while/body/eval_jaxpr/dot_general | solution.py:34
  58.7 0.1 select_add_fusion.4
  59.0 3.0 %fusion.44 = f32[32,2048]{1,0:T(8,128)S(1)} fusion(bf16[1024,2048]{1,0:T(8,128)(2,1)} %get-tuple-element.192, bf16[32,512]{1,0:T(8,128)(2,1)S(1)} %get-tuple-element.163, bf16[32,512]{1,0:T(8,128)(2,1)S(1)} %get-tuple-element.164), kind=kOutput, calls=%fused_computation.4.clone.1 | convolution fusion | flops 134348800 | bytes 4521984 | tf_op jit(solution)/shard_map/while/body/eval_jaxpr/dot_general | solution.py:34
  62.0 0.1 select_add_fusion.4
  62.3 3.0 %fusion.44 = f32[32,2048]{1,0:T(8,128)S(1)} fusion(bf16[1024,2048]{1,0:T(8,128)(2,1)} %get-tuple-element.192, bf16[32,512]{1,0:T(8,128)(2,1)S(1)} %get-tuple-element.163, bf16[32,512]{1,0:T(8,128)(2,1)S(1)} %get-tuple-element.164), kind=kOutput, calls=%fused_computation.4.clone.1 | convolution fusion | flops 134348800 | bytes 4521984 | tf_op jit(solution)/shard_map/while/body/eval_jaxpr/dot_general | solution.py:34
  65.3 0.1 select_add_fusion.4
  65.6 3.0 %fusion.44 = f32[32,2048]{1,0:T(8,128)S(1)} fusion(bf16[1024,2048]{1,0:T(8,128)(2,1)} %get-tuple-element.192, bf16[32,512]{1,0:T(8,128)(2,1)S(1)} %get-tuple-element.163, bf16[32,512]{1,0:T(8,128)(2,1)S(1)} %get-tuple-element.164), kind=kOutput, calls=%fused_computation.4.clone.1 | convolution fusion | flops 134348800 | bytes 4521984 | tf_op jit(solution)/shard_map/while/body/eval_jaxpr/dot_general | solution.py:34
  68.7 0.1 select_add_fusion.4
  69.0 3.0 %fusion.44 = f32[32,2048]{1,0:T(8,128)S(1)} fusion(bf16[1024,2048]{1,0:T(8,128)(2,1)} %get-tuple-element.192, bf16[32,512]{1,0:T(8,128)(2,1)S(1)} %get-tuple-element.163, bf16[32,512]{1,0:T(8,128)(2,1)S(1)} %get-tuple-element.164), kind=kOutput, calls=%fused_computation.4.clone.1 | convolution fusion | flops 134348800 | bytes 4521984 | tf_op jit(solution)/shard_map/while/body/eval_jaxpr/dot_general | solution.py:34
  72.0 0.1 select_add_fusion.4
  72.3 3.0 %fusion.44 = f32[32,2048]{1,0:T(8,128)S(1)} fusion(bf16[1024,2048]{1,0:T(8,128)(2,1)} %get-tuple-element.192, bf16[32,512]{1,0:T(8,128)(2,1)S(1)} %get-tuple-element.163, bf16[32,512]{1,0:T(8,128)(2,1)S(1)} %get-tuple-element.164), kind=kOutput, calls=%fused_computation.4.clone.1 | convolution fusion | flops 134348800 | bytes 4521984 | tf_op jit(solution)/shard_map/while/body/eval_jaxpr/dot_general | solution.py:34
  75.3 0.1 select_add_fusion.4
  75.6 3.0 %fusion.44 = f32[32,2048]{1,0:T(8,128)S(1)} fusion(bf16[1024,2048]{1,0:T(8,128)(2,1)} %get-tuple-element.192, bf16[32,512]{1,0:T(8,128)(2,1)S(1)} %get-tuple-element.163, bf16[32,512]{1,0:T(8,128)(2,1)S(1)} %get-tuple-element.164), kind=kOutput, calls=%fused_computation.4.clone.1 | convolution fusion | flops 134348800 | bytes 4521984 | tf_op jit(solution)/shard_map/while/body/eval_jaxpr/dot_general | solution.py:34
  78.9 3.0 %fusion.44 = f32[32,2048]{1,0:T(8,128)S(1)} fusion(bf16[1024,2048]{1,0:T(8,128)(2,1)} %get-tuple-element.192, bf16[32,512]{1,0:T(8,128)(2,1)S(1)} %get-tuple-element.163, bf16[32,512]{1,0:T(8,128)(2,1)S(1)} %get-tuple-element.164), kind=kOutput, calls=%fused_computation.4.clone.1 | convolution fusion | flops 134348800 | bytes 4521984 | tf_op jit(solution)/shard_map/while/body/eval_jaxpr/dot_general | solution.py:34
  82.2 3.0 %fusion.44 = f32[32,2048]{1,0:T(8,128)S(1)} fusion(bf16[1024,2048]{1,0:T(8,128)(2,1)} %get-tuple-element.192, bf16[32,512]{1,0:T(8,128)(2,1)S(1)} %get-tuple-element.163, bf16[32,512]{1,0:T(8,128)(2,1)S(1)} %get-tuple-element.164), kind=kOutput, calls=%fused_computation.4.clone.1 | convolution fusion | flops 134348800 | bytes 4521984 | tf_op jit(solution)/shard_map/while/body/eval_jaxpr/dot_general | solution.py:34
  85.5 3.0 %fusion.44 = f32[32,2048]{1,0:T(8,128)S(1)} fusion(bf16[1024,2048]{1,0:T(8,128)(2,1)} %get-tuple-element.192, bf16[32,512]{1,0:T(8,128)(2,1)S(1)} %get-tuple-element.163, bf16[32,512]{1,0:T(8,128)(2,1)S(1)} %get-tuple-element.164), kind=kOutput, calls=%fused_computation.4.clone.1 | convolution fusion | flops 134348800 | bytes 4521984 | tf_op jit(solution)/shard_map/while/body/eval_jaxpr/dot_general | solution.py:34
  88.9 3.0 %fusion.44 = f32[32,2048]{1,0:T(8,128)S(1)} fusion(bf16[1024,2048]{1,0:T(8,128)(2,1)} %get-tuple-element.192, bf16[32,512]{1,0:T(8,128)(2,1)S(1)} %get-tuple-element.163, bf16[32,512]{1,0:T(8,128)(2,1)S(1)} %get-tuple-element.164), kind=kOutput, calls=%fused_computation.4.clone.1 | convolution fusion | flops 134348800 | bytes 4521984 | tf_op jit(solution)/shard_map/while/body/eval_jaxpr/dot_general | solution.py:34
  92.0 0.6 copy-done
  93.1 0.6 dynamic-slice
  94.3 0.3 fusion.14
  94.6 21.6 %all-reduce.6.cloned.1.call-done = (f32[4,8,1024]{2,1,0:T(8,128)}, f32[4,8,1024]{2,1,0:T(8,128)}, f32[4,8,1024]{2,1,0:T(8,128)}) async-done(((f32[4,8,1024]{2,1,0:T(8,128)}, f32[4,8,1024]{2,1,0:T(8,128)}, f32[4,8,1024]{2,1,0:T(8,128)}), (f32[4,8,1024]{2,1,0:T(8,128)}, f32[4,8,1024]{2,1,0:T(8,128)}, f32[4,8,1024]{2,1,0:T(8,128)})) %all-reduce.6.cloned.1.call-update) | async-done | bytes 393232
  116.3 1.1 fusion.22
  117.4 0.7 reshape.50
  118.1 0.7 reshape.53
  (112 shorter events, 2.3 us)
Async XLA Ops:
  7.2 17.6 %copy-start.3 = (f32[12,2,1024]{2,1,0:T(2,128)S(1)}, f32[12,2,1024]{2,1,0:T(2,128)}, u32[]{:S(2)}) copy-start(f32[12,2,1024]{2,1,0:T(2,128)} %param.5) | copy-start | bytes 294916
  7.2 109.1 %all-reduce.6.cloned.1.call-start = ((), (), s32[]{:S(2)}) async-start(), calls=%async_computation | async-start | bytes 786432
  52.2 40.6 %copy-start.4 = (s32[16]{0:T(128)S(1)}, s32[16]{0:T(128)}, u32[]{:S(2)}) copy-start(s32[16]{0:T(128)} %param.6) | copy-start | bytes 196
  52.2 40.9 %copy-start.6 = (u32[32]{0:T(128)S(1)}, u32[32]{0:T(128)}, u32[]{:S(2)}) copy-start(u32[32]{0:T(128)} %constant.76) | copy-start | bytes 388
  52.2 42.1 %copy-start.5 = (s32[16,16]{1,0:T(8,128)S(1)}, s32[16,16]{1,0:T(8,128)}, u32[]{:S(2)}) copy-start(s32[16,16]{1,0:T(8,128)} %param.7) | copy-start | bytes 3076
  92.0 0.6 copy-start
  92.0 0.7 copy-start.1
  92.0 0.7 copy-start.2
Sparse Core Ops, SparseCore 0:
  92.9 23.3 all-reduce.5
where the time goes:
time: 126 us
  matrix products  36.4 us (29%)
  other arithmetic  28.1 us (22%)
  waiting for transfers between devices  21.6 us (17%)
  blocking collectives  19.8 us (16%)
  between operations  14.8 us (12%)
  local copies, waits for them, and re-layouts  3.89 us (3%)
    dot_general x12, matrix products, window_terms(): jnp.dot(cross_spectra, transform, preferred_element_type=jnp.float32)  36.1 us
    unnamed x2, waiting for transfers between devices  21.6 us
    all_gather x1, blocking collectives, on_device(): col_side = lax.all_gather(spectra, 'row', axis=1, tiled=True)  15.3 us
    sin x1, other arithmetic, build_transform(): sine_values = jnp.sin(angles)  9.01 us
    neg x1, other arithmetic, build_transform(): lower_half = jnp.concatenate([-sine_values, cosine_values], 1)  8.58 us
    convert_element_type x1, other arithmetic, build_transform(): return (jnp.concatenate([upper_half, lower_half], 0) * (1.0 / (3.0 * math...  7.58 us
    all_gather x1, blocking collectives, on_device(): row_side = lax.all_gather(spectra, 'col', axis=1, tiled=True)  4.48 us
  transfers between devices with their start and end apart: 1, of which 1 were waited for; matrix products, arithmetic and copies ran while one was open for 1% of the time, Pallas kernels for 0%

commit v1 on v0

v1 whole, which is shorter than its diff:
```python
import functools
import math

import jax
import jax.numpy as jnp
import ml_dtypes
import numpy as np
from jax import lax
from jax.experimental import pallas as pl
from jax.experimental.pallas import tpu as pltpu
from jax.sharding import PartitionSpec as P

MESH = pl.DeviceIdType.MESH


def transform_table(bin_count):
    lag_count = 2 * bin_count
    phase_index = np.arange(bin_count)[:, None] * np.arange(lag_count)[None, :] % lag_count
    angles = phase_index * (2.0 * math.pi / lag_count)
    cosine, sine = np.cos(angles), np.sin(angles)
    table = np.concatenate(
        [np.concatenate([cosine, sine], 1), np.concatenate([-sine, cosine], 1)], 0
    )
    table = table / (3.0 * math.sqrt(bin_count))
    return table.astype(np.float32).astype(ml_dtypes.bfloat16)


def kernel(
    n_row, n_col, owned, labels_ref, mask_ref, spectra_ref, table_hbm, linear_ref, phase_ref,
    blocks, table, cross, table_sem, send_sem, recv_sem,
):
    half = n_row // 2
    row, col, core = lax.axis_index("row"), lax.axis_index("col"), lax.axis_index("tm")
    windows_here = spectra_ref.shape[0]
    rows = windows_here * owned
    bins = spectra_ref.shape[2] // 2
    lags = 2 * bins
    windows = 2 * windows_here
    base = core * half
    other = 1 - core
    home = row // half
    lane = row % half

    table_copy = pltpu.make_async_copy(table_hbm, table, table_sem)
    table_copy.start()

    barrier = pltpu.get_barrier_semaphore()
    pl.semaphore_signal(barrier, inc=1, device_id={"tm": other}, device_id_type=MESH)
    for step in range(1, n_col):
        for t in range(2):
            pl.semaphore_signal(
                barrier, inc=1, device_id={"col": (col + step) % n_col, "tm": t},
                device_id_type=MESH,
            )
    for a in range(half):
        @pl.when(base + a != row)
        def _():
            for t in range(2):
                pl.semaphore_signal(
                    barrier, inc=1, device_id={"row": base + a, "tm": t}, device_id_type=MESH
                )

    blocks[col, core] = spectra_ref[...].reshape(rows, 2 * bins)
    pl.semaphore_wait(barrier, 1 + 2 * (n_col - 1) + (n_row - 1))

    mine = blocks.at[col, core]
    copies = []

    def send(slot, where):
        copy = pltpu.make_async_remote_copy(
            src_ref=mine, dst_ref=blocks.at[slot, core], send_sem=send_sem.at[len(copies)],
            recv_sem=recv_sem.at[slot, core], device_id=where, device_id_type=MESH,
        )
        copy.start()
        copies.append(copy)

    for step in sorted(range(1, n_row), key=lambda s: abs(s - half)):
        send(n_col + lane, {"row": (row + step) % n_row, "tm": home})
    for step in range(1, n_col):
        for t in range(2):
            send(col, {"col": (col + step) % n_col, "tm": t})
    send(col, {"tm": other})

    def arrived(slot, h):
        pltpu.make_async_copy(mine, blocks.at[slot, h], recv_sem.at[slot, h]).wait()

    arrived(col, other)
    for step in range(1, n_col):
        for h in range(2):
            arrived((col + step) % n_col, h)

    odd = lax.broadcasted_iota(jnp.int32, (rows, 2 * bins), 0) % 2 == 1
    start = jnp.clip(row - base, 0, half - 1)
    group_rows = lax.broadcasted_iota(jnp.int32, (8, 1), 0)

    def one_row(index, carry):
        a = (start + index) % half
        away = base + a != row
        slot = jnp.where(away, n_col + a, col)

        @pl.when(away)
        def _():
            for h in range(2):
                arrived(n_col + a, h)

        for h in range(2):
            right = blocks[slot, h]
            right_real, right_imag = right[:, :bins], right[:, bins:]
            for c in range(n_col):
                left = blocks[c, h]
                for s in range(2):
                    if s:
                        left = jnp.where(
                            odd, pltpu.roll(left, 1, 0), pltpu.roll(left, rows - 1, 0)
                        )
                    left_real, left_imag = left[:, :bins], left[:, bins:]
                    at = pl.ds(((h * n_col + c) * 2 + s) * rows, rows)
                    cross[at, :bins] = (
                        left_real * right_real + left_imag * right_imag
                    ).astype(jnp.bfloat16)
                    cross[at, bins:] = (
                        left_imag * right_real - left_real * right_imag
                    ).astype(jnp.bfloat16)

        @pl.when(index == 0)
        def _():
            table_copy.wait()

        scales = []
        for pair in range(n_col // 2):
            scale = jnp.zeros((8, 1), jnp.float32)
            for p in range(8):
                first = labels_ref[row * n_col * owned + pair * 4 + p // 2]
                second = labels_ref[((base + a) * n_col + col) * owned + p % 2]
                kept = mask_ref[first, second].astype(jnp.float32)
                scale = jnp.where(group_rows == p, kept, scale)
            scales.append(scale)

        tile = 256

        def one_tile(j, carry):
            at = pl.ds(pl.multiple_of(j * tile, tile), tile)
            at_imag = pl.ds(pl.multiple_of(lags + j * tile, tile), tile)
            real = jnp.dot(cross[...], table[:, at], preferred_element_type=jnp.float32)
            imag = jnp.dot(cross[...], table[:, at_imag], preferred_element_type=jnp.float32)
            inverse = jnp.minimum(lax.rsqrt(real * real + imag * imag), 2.0)

            def total(part):
                part = part.reshape(2, n_col, 2, rows // 8, 8, tile).sum(axis=(0, 3))
                out = []
                for pair in range(n_col // 2):
                    whole = []
                    for s in range(2):
                        upper, lower = part[2 * pair, s], part[2 * pair + 1, s]
                        upper = upper + pltpu.roll(upper, 4, 0)
                        lower = lower + pltpu.roll(lower, 4, 0)
                        both = jnp.where(group_rows < 4, upper, lower)
                        whole.append(
                            both
                            + jnp.where(
                                group_rows % 4 < 2, pltpu.roll(both, 6, 0), pltpu.roll(both, 2, 0)
                            )
                        )
                    straight = (group_rows % 4 == 0) | (group_rows % 4 == 3)
                    out.append(jnp.where(straight, whole[0], whole[1]))
                return out

            stack, phase_real, phase_imag = total(real), total(real * inverse), total(imag * inverse)
            for pair in range(n_col // 2):
                linear = stack[pair] * scales[pair] * (1.0 / windows)
                power = phase_real[pair] * phase_real[pair] + phase_imag[pair] * phase_imag[pair]
                linear_ref[a, pl.ds(8 * pair, 8), at] = linear
                phase_ref[a, pl.ds(8 * pair, 8), at] = linear * power * (1.0 / (windows * windows))
            return carry

        lax.fori_loop(0, lags // tile, one_tile, 0)
        return carry

    lax.fori_loop(0, half, one_row, 0)

    for copy in copies:
        copy.wait_send()


def on_device(n_row, n_col, table, spectra, station_block, pair_mask):
    windows_here, owned, width = spectra.shape
    half = n_row // 2
    rows = windows_here * owned
    lags = width
    first = n_col * owned
    shape = jax.ShapeDtypeStruct((half, first * owned, lags), jnp.float32)
    sends = 1 + 2 * (n_col - 1) + (n_row - 1)
    linear, phase = pl.pallas_call(
        functools.partial(kernel, n_row, n_col, owned),
        out_shape=(shape, shape),
        in_specs=[
            pl.BlockSpec(memory_space=pltpu.SMEM),
            pl.BlockSpec(memory_space=pltpu.SMEM),
            pl.BlockSpec(memory_space=pltpu.VMEM),
            pl.BlockSpec(memory_space=pl.ANY),
        ],
        out_specs=[pl.BlockSpec(memory_space=pltpu.VMEM)] * 2,
        scratch_shapes=[
            pltpu.VMEM((n_col + half, 2, rows, width), jnp.float32),
            pltpu.VMEM(table.shape, jnp.bfloat16),
            pltpu.VMEM((4 * n_col * rows, width), jnp.bfloat16),
            pltpu.SemaphoreType.DMA,
            pltpu.SemaphoreType.DMA((sends,)),
            pltpu.SemaphoreType.DMA((n_col + half, 2)),
        ],
        compiler_params=pltpu.CompilerParams(
            collective_id=0, has_side_effects=True, vmem_limit_bytes=48 * 1024 * 1024
        ),
    )(station_block, pair_mask, spectra, jnp.asarray(table))

    def placed(part):
        part = part.reshape(half, first, owned, lags)
        return part.transpose(1, 0, 2, 3)[:, :, None]

    return placed(linear), placed(phase)


def solution(mesh):
    def program(spectra, station_block, pair_mask):
        table = transform_table(spectra.shape[2] // 2)
        in_specs = (P("tm", ("group", "row", "col"), None), P("group"), P("group", None))
        out_specs = (
            P(("group", "row"), "tm", "col", None, None),
            P(("group", "row"), "tm", "col", None, None),
        )
        return jax.shard_map(
            functools.partial(on_device, mesh.shape["row"], mesh.shape["col"], table),
            mesh=mesh, in_specs=in_specs, out_specs=out_specs, check_vma=False,
        )(spectra, station_block, pair_mask)

    return program
```

time: 126 us -> 23.8 us (0.19)
  matrix products: 36.4 us -> 0 us
  other arithmetic: 28.1 us -> 0 us
  waiting for transfers between devices: 21.6 us -> 0 us
  blocking collectives: 19.8 us -> 0 us
  Pallas kernels: 0 us -> 17.7 us
  between operations: 14.8 us -> 0.66 us
  local copies, waits for them, and re-layouts: 3.89 us -> 5.17 us
    dot_general x13 -> x0, matrix products: 36.4 us -> none  [the longest x12 36.1 us: window_terms(): jnp.dot(cross_spectra, transform, preferred_element_type=jnp.float32)]
    unnamed x2 -> x0, waiting for transfers between devices: 21.6 us -> none
    all_gather x2 -> x0, blocking collectives: 19.8 us -> none  [the longest x1 15.3 us: on_device(): col_side = lax.all_gather(spectra, 'row', axis=1, tiled=True)]
    pallas_call x0 -> x1, Pallas kernels: none -> 17.7 us  [on_device(): pl.pallas_call(functools.partial(kernel, n_row, n_col, owned), out_shape=...]
    sin x1 -> x0, other arithmetic: 9.01 us -> none  [build_transform(): sine_values = jnp.sin(angles)]
    neg x1 -> x0, other arithmetic: 8.58 us -> none  [build_transform(): lower_half = jnp.concatenate([-sine_values, cosine_values], 1)]
    convert_element_type x1 -> x0, other arithmetic: 7.58 us -> none  [build_transform(): return (jnp.concatenate([upper_half, lower_half], 0) * (1.0 / (3.0 * math...]
    unnamed x16 -> x8, local copies, waits for them, and re-layouts: 1.36 us -> 4.43 us
  transfers between devices with their start and end apart: 1 -> 0, of which waited for: 1 -> 0; matrix products, arithmetic and copies ran while one was open for 1% -> 0% of each run, Pallas kernels for 0% -> 0%
where the time goes in v1:
time: 23.8 us; the launch traced here: 23.6 us
  Pallas kernels  17.7 us (74%)
  local copies, waits for them, and re-layouts  5.17 us (22%)
  between operations  0.66 us (3%)
    pallas_call x1, Pallas kernels, on_device(): pl.pallas_call(functools.partial(kernel, n_row, n_col, owned), out_shape=...  17.7 us
    unnamed x8, local copies, waits for them, and re-layouts  4.43 us
    broadcast_in_dim x1, local copies, waits for them, and re-layouts, placed(): return part.transpose(1, 0, 2, 3)[:, :, None]  0.66 us

profile of v1, /device:TPU:1, one launch (start us, length us, event | category | flops | bytes accessed | tf_op | source)
XLA Modules:
  0.0 23.6 jit_solution(13312087847835482858)
XLA Ops:
  0.6 0.0 copy-start
  0.6 2.2 %copy-done = bf16[1024,2048]{1,0:T(8,128)(2,1)S(1)} copy-done((bf16[1024,2048]{1,0:T(8,128)(2,1)S(1)}, bf16[1024,2048]{1,0:T(8,128)(2,1)}, u32[]{:S(2)}) %copy-start) | copy-done | bytes 4194328
  2.8 0.0 copy-start.1
  2.8 0.9 %copy-done.1 = f32[12,2,1024]{2,1,0:T(2,128)S(1)} copy-done((f32[12,2,1024]{2,1,0:T(2,128)S(1)}, f32[12,2,1024]{2,1,0:T(2,128)}, u32[]{:S(2)}) %copy-start.1) | copy-done | bytes 98328
  3.7 0.0 copy-start.2
  3.7 0.7 %copy-done.2 = s32[16,16]{1,0:T(8,128)S(1)} copy-done((s32[16,16]{1,0:T(8,128)S(1)}, s32[16,16]{1,0:T(8,128)}, u32[]{:S(2)}) %copy-start.2) | copy-done | bytes 1048
  4.4 0.0 copy-start.3
  4.4 0.7 %copy-done.3 = s32[16]{0:T(128)S(1)} copy-done((s32[16]{0:T(128)S(1)}, s32[16]{0:T(128)}, u32[]{:S(2)}) %copy-start.3) | copy-done | bytes 88
  5.1 17.7 %shard_map.59 = (f32[2,8,1024]{2,1,0:T(8,128)S(1)}, f32[2,8,1024]{2,1,0:T(8,128)S(1)}) custom-call(s32[16]{0:T(128)S(1)} %copy-done.3, s32[16,16]{1,0:T(8,128)S(1)} %copy-done.2, f32[12,2,1024]{2,1,0:T(2,128)S(1)} %copy-done.1, bf16[1024,2048]{1,0:T(8,128)(2,1)S(1)} %copy-done), custom_call_target="tpu_custom_call" | custom-call | tf_op jit(solution)/shard_map/pallas_call | solution.py:193
  22.9 0.7 %copy_bitcast_fusion = (f32[4,2,1,2,1024]{4,3,2,1,0:T(2,128)}, f32[4,2,1,2,1024]{4,3,2,1,0:T(2,128)}) fusion(f32[2,4,2,1024]{3,2,1,0:T(2,128)S(1)} %reshape.11, f32[2,4,2,1024]{3,2,1,0:T(2,128)S(1)} %reshape.10), kind=kLoop, calls=%fused_computation | loop fusion | bytes 262144 | tf_op jit(solution)/shard_map/broadcast_in_dim | solution.py:218
  (2 shorter events, 0.1 us)
Async XLA Ops:
  0.6 2.2 %copy-start = (bf16[1024,2048]{1,0:T(8,128)(2,1)S(1)}, bf16[1024,2048]{1,0:T(8,128)(2,1)}, u32[]{:S(2)}) copy-start(bf16[1024,2048]{1,0:T(8,128)(2,1)} %constant.2.clone.table_hbm) | copy-start | bytes 12582916
  2.8 0.9 %copy-start.1 = (f32[12,2,1024]{2,1,0:T(2,128)S(1)}, f32[12,2,1024]{2,1,0:T(2,128)}, u32[]{:S(2)}) copy-start(f32[12,2,1024]{2,1,0:T(2,128)} %spectra_ref.1) | copy-start | bytes 294916
  3.7 0.7 %copy-start.2 = (s32[16,16]{1,0:T(8,128)S(1)}, s32[16,16]{1,0:T(8,128)}, u32[]{:S(2)}) copy-start(s32[16,16]{1,0:T(8,128)} %mask_ref.1) | copy-start | bytes 3076
  4.4 0.7 %copy-start.3 = (s32[16]{0:T(128)S(1)}, s32[16]{0:T(128)}, u32[]{:S(2)}) copy-start(s32[16]{0:T(128)} %labels_ref.1) | copy-start | bytes 196

commit v2 on v1

--- a/solution.py
+++ b/solution.py
@@ -26,8 +26,8 @@
 
 
 def kernel(
-    n_row, n_col, owned, labels_ref, mask_ref, spectra_ref, table_hbm, linear_ref, phase_ref,
-    blocks, table, cross, table_sem, send_sem, recv_sem,
+    n_row, n_col, owned, labels_hbm, mask_hbm, spectra_hbm, table_hbm, linear_ref, phase_ref,
+    blocks, table, cross, spectra_ref, labels_ref, mask_ref, local_sem, send_sem, recv_sem,
 ):
     half = n_row // 2
     row, col, core = lax.axis_index("row"), lax.axis_index("col"), lax.axis_index("tm")
@@ -41,7 +41,13 @@
     home = row // half
     lane = row % half
 
-    table_copy = pltpu.make_async_copy(table_hbm, table, table_sem)
+    spectra_copy = pltpu.make_async_copy(spectra_hbm, spectra_ref, local_sem.at[0])
+    spectra_copy.start()
+    labels_copy = pltpu.make_async_copy(labels_hbm, labels_ref, local_sem.at[1])
+    labels_copy.start()
+    mask_copy = pltpu.make_async_copy(mask_hbm, mask_ref, local_sem.at[2])
+    mask_copy.start()
+    table_copy = pltpu.make_async_copy(table_hbm, table, local_sem.at[3])
     table_copy.start()
 
     barrier = pltpu.get_barrier_semaphore()
@@ -60,6 +66,7 @@
                     barrier, inc=1, device_id={"row": base + a, "tm": t}, device_id_type=MESH
                 )
 
+    spectra_copy.wait()
     blocks[col, core] = spectra_ref[...].reshape(rows, 2 * bins)
     pl.semaphore_wait(barrier, 1 + 2 * (n_col - 1) + (n_row - 1))
 
@@ -84,6 +91,8 @@
     def arrived(slot, h):
         pltpu.make_async_copy(mine, blocks.at[slot, h], recv_sem.at[slot, h]).wait()
 
+    labels_copy.wait()
+    mask_copy.wait()
     arrived(col, other)
     for step in range(1, n_col):
         for h in range(2):
@@ -173,7 +182,7 @@
                 phase_ref[a, pl.ds(8 * pair, 8), at] = linear * power * (1.0 / (windows * windows))
             return carry
 
-        lax.fori_loop(0, lags // tile, one_tile, 0)
+        lax.fori_loop(0, lags // tile, one_tile, 0, unroll=True)
         return carry
 
     lax.fori_loop(0, half, one_row, 0)
@@ -188,30 +197,35 @@
     rows = windows_here * owned
     lags = width
     first = n_col * owned
-    shape = jax.ShapeDtypeStruct((half, first * owned, lags), jnp.float32)
+    shape = pltpu.VMEM((half, first * owned, lags), jnp.float32)
     sends = 1 + 2 * (n_col - 1) + (n_row - 1)
     linear, phase = pl.pallas_call(
         functools.partial(kernel, n_row, n_col, owned),
         out_shape=(shape, shape),
         in_specs=[
-            pl.BlockSpec(memory_space=pltpu.SMEM),
-            pl.BlockSpec(memory_space=pltpu.SMEM),
-            pl.BlockSpec(memory_space=pltpu.VMEM),
-            pl.BlockSpec(memory_space=pl.ANY),
-        ],
+            pl.BlockSpec(memory_space=pltpu.HBM),
+        ] * 4,
         out_specs=[pl.BlockSpec(memory_space=pltpu.VMEM)] * 2,
         scratch_shapes=[
             pltpu.VMEM((n_col + half, 2, rows, width), jnp.float32),
             pltpu.VMEM(table.shape, jnp.bfloat16),
             pltpu.VMEM((4 * n_col * rows, width), jnp.bfloat16),
-            pltpu.SemaphoreType.DMA,
+            pltpu.VMEM(spectra.shape, jnp.float32),
+            pltpu.SMEM(station_block.shape, jnp.int32),
+            pltpu.SMEM(pair_mask.shape, jnp.int32),
+            pltpu.SemaphoreType.DMA((4,)),
             pltpu.SemaphoreType.DMA((sends,)),
             pltpu.SemaphoreType.DMA((n_col + half, 2)),
         ],
         compiler_params=pltpu.CompilerParams(
             collective_id=0, has_side_effects=True, vmem_limit_bytes=48 * 1024 * 1024
         ),
-    )(station_block, pair_mask, spectra, jnp.asarray(table))
+    )(
+        *(
+            pltpu.with_memory_space_constraint(part, pltpu.HBM)
+            for part in (station_block, pair_mask, spectra, jnp.asarray(table))
+        )
+    )
 
     def placed(part):
         part = part.reshape(half, first, owned, lags)

time: 23.8 us -> 17.2 us (0.72)
  local copies, waits for them, and re-layouts: 5.17 us -> 0.74 us
  Pallas kernels: 17.7 us -> 15.6 us
    unnamed x8 -> x0, local copies, waits for them, and re-layouts: 4.43 us -> none
    pallas_call x1, Pallas kernels: 17.7 us -> 15.6 us  [on_device(): pl.pallas_call(functools.partial(kernel, n_row, n_col, owned), out_shape=...]
where the time goes in v2:
time: 17.2 us; the launch traced here: 17 us
  Pallas kernels  15.6 us (91%)
  local copies, waits for them, and re-layouts  0.74 us (4%)
  between operations  0.65 us (4%)
    pallas_call x1, Pallas kernels, on_device(): pl.pallas_call(functools.partial(kernel, n_row, n_col, owned), out_shape=...  15.6 us
    broadcast_in_dim x1, local copies, waits for them, and re-layouts, placed(): return part.transpose(1, 0, 2, 3)[:, :, None]  0.66 us

profile of v2, /device:TPU:1, one launch (start us, length us, event | category | flops | bytes accessed | tf_op | source)
XLA Modules:
  0.0 17.0 jit_solution(3932509385619960593)
XLA Ops:
  0.6 15.6 %shard_map.59 = (f32[2,8,1024]{2,1,0:T(8,128)S(1)}, f32[2,8,1024]{2,1,0:T(8,128)S(1)}) custom-call(s32[16]{0:T(128)} %labels_hbm.1, s32[16,16]{1,0:T(8,128)} %mask_hbm.1, f32[12,2,1024]{2,1,0:T(2,128)} %spectra_hbm.1, bf16[1024,2048]{1,0:T(8,128)(2,1)} %constant.2.clone.table_hbm), custom_call_target="tpu_custom_call" | custom-call | tf_op jit(solution)/shard_map/pallas_call | solution.py:202
  16.4 0.7 %copy_bitcast_fusion = (f32[4,2,1,2,1024]{4,3,2,1,0:T(2,128)}, f32[4,2,1,2,1024]{4,3,2,1,0:T(2,128)}) fusion(f32[2,4,2,1024]{3,2,1,0:T(2,128)S(1)} %reshape.11, f32[2,4,2,1024]{3,2,1,0:T(2,128)S(1)} %reshape.10), kind=kLoop, calls=%fused_computation | loop fusion | bytes 262144 | tf_op jit(solution)/shard_map/broadcast_in_dim | solution.py:232
  (2 shorter events, 0.1 us)

commit v3 on v2

--- a/solution.py
+++ b/solution.py
@@ -27,7 +27,7 @@
 
 def kernel(
     n_row, n_col, owned, labels_hbm, mask_hbm, spectra_hbm, table_hbm, linear_ref, phase_ref,
-    blocks, table, cross, spectra_ref, labels_ref, mask_ref, local_sem, send_sem, recv_sem,
+    blocks, swapped, table, cross, spectra_ref, labels_ref, mask_ref, local_sem, send_sem, recv_sem,
 ):
     half = n_row // 2
     row, col, core = lax.axis_index("row"), lax.axis_index("col"), lax.axis_index("tm")
@@ -99,6 +99,11 @@
             arrived((col + step) % n_col, h)
 
     odd = lax.broadcasted_iota(jnp.int32, (rows, 2 * bins), 0) % 2 == 1
+    for h in range(2):
+        for c in range(n_col):
+            left = blocks[c, h]
+            swapped[c, h] = jnp.where(odd, pltpu.roll(left, 1, 0), pltpu.roll(left, rows - 1, 0))
+    table_copy.wait()
     start = jnp.clip(row - base, 0, half - 1)
     group_rows = lax.broadcasted_iota(jnp.int32, (8, 1), 0)
 
@@ -106,34 +111,6 @@
         a = (start + index) % half
         away = base + a != row
         slot = jnp.where(away, n_col + a, col)
-
-        @pl.when(away)
-        def _():
-            for h in range(2):
-                arrived(n_col + a, h)
-
-        for h in range(2):
-            right = blocks[slot, h]
-            right_real, right_imag = right[:, :bins], right[:, bins:]
-            for c in range(n_col):
-                left = blocks[c, h]
-                for s in range(2):
-                    if s:
-                        left = jnp.where(
-                            odd, pltpu.roll(left, 1, 0), pltpu.roll(left, rows - 1, 0)
-                        )
-                    left_real, left_imag = left[:, :bins], left[:, bins:]
-                    at = pl.ds(((h * n_col + c) * 2 + s) * rows, rows)
-                    cross[at, :bins] = (
-                        left_real * right_real + left_imag * right_imag
-                    ).astype(jnp.bfloat16)
-                    cross[at, bins:] = (
-                        left_imag * right_real - left_real * right_imag
-                    ).astype(jnp.bfloat16)
-
-        @pl.when(index == 0)
-        def _():
-            table_copy.wait()
 
         scales = []
         for pair in range(n_col // 2):
@@ -145,7 +122,29 @@
                 scale = jnp.where(group_rows == p, kept, scale)
             scales.append(scale)
 
-        tile = 256
+        @pl.when(away)
+        def _():
+            for h in range(2):
+                arrived(n_col + a, h)
+
+        for h in range(2):
+            right = blocks[slot, h]
+            right_real, right_imag = right[:, :bins], right[:, bins:]
+            for c in range(n_col):
+                left = blocks[c, h]
+                for s in range(2):
+                    if s:
+                        left = swapped[c, h]
+                    left_real, left_imag = left[:, :bins], left[:, bins:]
+                    at = pl.ds(((h * n_col + c) * 2 + s) * rows, rows)
+                    cross[at, :bins] = (
+                        left_real * right_real + left_imag * right_imag
+                    ).astype(jnp.bfloat16)
+                    cross[at, bins:] = (
+                        left_imag * right_real - left_real * right_imag
+                    ).astype(jnp.bfloat16)
+
+        tile = 512
 
         def one_tile(j, carry):
             at = pl.ds(pl.multiple_of(j * tile, tile), tile)
@@ -208,6 +207,7 @@
         out_specs=[pl.BlockSpec(memory_space=pltpu.VMEM)] * 2,
         scratch_shapes=[
             pltpu.VMEM((n_col + half, 2, rows, width), jnp.float32),
+            pltpu.VMEM((n_col, 2, rows, width), jnp.float32),
             pltpu.VMEM(table.shape, jnp.bfloat16),
             pltpu.VMEM((4 * n_col * rows, width), jnp.bfloat16),
             pltpu.VMEM(spectra.shape, jnp.float32),

time: 17.2 us -> 16.8 us (0.977)
  Pallas kernels: 15.6 us -> 15.3 us
    pallas_call x1, Pallas kernels: 15.6 us -> 15.3 us  [on_device(): pl.pallas_call(functools.partial(kernel, n_row, n_col, owned), out_shape=...]
where the time goes in v3:
time: 16.8 us; the launch traced here: 16.7 us
  Pallas kernels  15.3 us (91%)
  local copies, waits for them, and re-layouts  0.74 us (4%)
  between operations  0.65 us (4%)
    pallas_call x1, Pallas kernels, on_device(): pl.pallas_call(functools.partial(kernel, n_row, n_col, owned), out_shape=...  15.3 us
    broadcast_in_dim x1, local copies, waits for them, and re-layouts, placed(): return part.transpose(1, 0, 2, 3)[:, :, None]  0.66 us

profile of v3, /device:TPU:1, one launch (start us, length us, event | category | flops | bytes accessed | tf_op | source)
XLA Modules:
  0.0 16.7 jit_solution(6466394990811452303)
XLA Ops:
  0.6 15.3 %shard_map.59 = (f32[2,8,1024]{2,1,0:T(8,128)S(1)}, f32[2,8,1024]{2,1,0:T(8,128)S(1)}) custom-call(s32[16]{0:T(128)} %labels_hbm.1, s32[16,16]{1,0:T(8,128)} %mask_hbm.1, f32[12,2,1024]{2,1,0:T(2,128)} %spectra_hbm.1, bf16[1024,2048]{1,0:T(8,128)(2,1)} %constant.2.clone.table_hbm), custom_call_target="tpu_custom_call" | custom-call | tf_op jit(solution)/shard_map/pallas_call | solution.py:201
  16.0 0.7 %copy_bitcast_fusion = (f32[4,2,1,2,1024]{4,3,2,1,0:T(2,128)}, f32[4,2,1,2,1024]{4,3,2,1,0:T(2,128)}) fusion(f32[2,4,2,1024]{3,2,1,0:T(2,128)S(1)} %reshape.11, f32[2,4,2,1024]{3,2,1,0:T(2,128)S(1)} %reshape.10), kind=kLoop, calls=%fused_computation | loop fusion | bytes 262144 | tf_op jit(solution)/shard_map/broadcast_in_dim | solution.py:232
  (2 shorter events, 0.1 us)

commit v4 on v3

--- a/solution.py
+++ b/solution.py
@@ -104,7 +104,7 @@
             left = blocks[c, h]
             swapped[c, h] = jnp.where(odd, pltpu.roll(left, 1, 0), pltpu.roll(left, rows - 1, 0))
     table_copy.wait()
-    start = jnp.clip(row - base, 0, half - 1)
+    start = lane
     group_rows = lax.broadcasted_iota(jnp.int32, (8, 1), 0)
 
     def one_row(index, carry):

time: 16.8 us -> 16.8 us (level)
  no operation moved by 1% of the time
where the time goes in v4:
time: 16.8 us; the launch traced here: 16.7 us
  Pallas kernels  15.3 us (91%)
  local copies, waits for them, and re-layouts  0.74 us (4%)
  between operations  0.65 us (4%)
    pallas_call x1, Pallas kernels, on_device(): pl.pallas_call(functools.partial(kernel, n_row, n_col, owned), out_shape=...  15.3 us
    broadcast_in_dim x1, local copies, waits for them, and re-layouts, placed(): return part.transpose(1, 0, 2, 3)[:, :, None]  0.66 us

profile of v4, /device:TPU:1, one launch (start us, length us, event | category | flops | bytes accessed | tf_op | source)
XLA Modules:
  0.0 16.7 jit_solution(14121440610251849595)
XLA Ops:
  0.6 15.3 %shard_map.59 = (f32[2,8,1024]{2,1,0:T(8,128)S(1)}, f32[2,8,1024]{2,1,0:T(8,128)S(1)}) custom-call(s32[16]{0:T(128)} %labels_hbm.1, s32[16,16]{1,0:T(8,128)} %mask_hbm.1, f32[12,2,1024]{2,1,0:T(2,128)} %spectra_hbm.1, bf16[1024,2048]{1,0:T(8,128)(2,1)} %constant.2.clone.table_hbm), custom_call_target="tpu_custom_call" | custom-call | tf_op jit(solution)/shard_map/pallas_call | solution.py:201
  16.0 0.7 %copy_bitcast_fusion = (f32[4,2,1,2,1024]{4,3,2,1,0:T(2,128)}, f32[4,2,1,2,1024]{4,3,2,1,0:T(2,128)}) fusion(f32[2,4,2,1024]{3,2,1,0:T(2,128)S(1)} %reshape.11, f32[2,4,2,1024]{3,2,1,0:T(2,128)S(1)} %reshape.10), kind=kLoop, calls=%fused_computation | loop fusion | bytes 262144 | tf_op jit(solution)/shard_map/broadcast_in_dim | solution.py:232
  (2 shorter events, 0.1 us)
